TPU v7x, 32 devices: a whole 2x2x4 slice. The times are simulated.
32 devices in a mesh: dp: 16 (over z, y, x), tensor: 2 (over core).
Axes of the slice: x: 2, y: 2, z: 4, core: 2. Of those that a mesh axis runs over, the one named last changes fastest.
Arguments:
- hidden_in: bfloat16 [32768, 768], P(('dp', 'tensor')), may hold values from -6 to 6
- out_grad: bfloat16 [32768, 768], P(('dp', 'tensor')), may hold values from -6 to 6
- seq_lengths: int32 [16, 8], P('dp'), may hold values from 1 to 1024, as said below
- attn_gain: bfloat16 [768], P('dp'), may hold values from 0.099609375 to 1.8984375
- attn_shift: bfloat16 [768], P('dp'), may hold values from -1.75 to 1.75
- mlp_gain: bfloat16 [768], P('dp'), may hold values from 0.099609375 to 1.8984375
- mlp_shift: bfloat16 [768], P('dp'), may hold values from -1.75 to 1.75
- qkv_weight: bfloat16 [768, 12, 192], P('dp', 'tensor'), may hold values from -0.21875 to 0.21875
- qkv_bias: bfloat16 [2304], P('dp'), may hold values from -1.75 to 1.75
- dense_weight: bfloat16 [768, 12, 64], P('dp', 'tensor'), may hold values from -0.875 to 0.875
- dense_bias: bfloat16 [768], P('dp'), may hold values from -1.75 to 1.75
- fc_weight: bfloat16 [768, 3072], P('dp', 'tensor'), may hold values from -0.21875 to 0.21875
- fc_bias: bfloat16 [3072], P('dp'), may hold values from -1.75 to 1.75
- proj_weight: bfloat16 [768, 3072], P('dp', 'tensor'), may hold values from -0.15625 to 0.15625
- proj_bias: bfloat16 [768], P('dp'), may hold values from -1.75 to 1.75
Outputs:
- block_out: bfloat16 [32768, 768], P(('dp', 'tensor'))
- input_grad: float32 [32768, 768], P(('dp', 'tensor'))
- attn_gain_grad: float32 [768], P(('dp', 'tensor'))
- attn_shift_grad: float32 [768], P(('dp', 'tensor'))
- mlp_gain_grad: float32 [768], P(('dp', 'tensor'))
- mlp_shift_grad: float32 [768], P(('dp', 'tensor'))
- qkv_weight_grad: float32 [768, 12, 192], P('dp', 'tensor')
- qkv_bias_grad: float32 [2304], P(('dp', 'tensor'))
- dense_weight_grad: float32 [768, 12, 64], P('dp', 'tensor')
- dense_bias_grad: float32 [768], P(('dp', 'tensor'))
- fc_weight_grad: float32 [768, 3072], P('dp', 'tensor')
- fc_bias_grad: float32 [3072], P(('dp', 'tensor'))
- proj_weight_grad: float32 [768, 3072], P('dp', 'tensor')
- proj_bias_grad: float32 [768], P(('dp', 'tensor'))
Inputs may be any that keep to these rules, and one draw needn't show every extreme that they name: `seq_lengths`: row g lists the 8 sequences of group g in order; they are all 1 or longer and sum to 2048. One sequence of each row has exactly 1024 rows and covers rows 1023 and 1024 of its group.
All inputs are finite; a program needn't handle non-finite values.
Results may differ from a plain program's by a relative error of at most 0.012.
Values may be sent and summed in bfloat16 or wider, within the bound.
A program may use at most 256 MiB of HBM per device.

v0:
```python
import jax
import jax.numpy as jnp
from jax import lax
from jax.sharding import PartitionSpec as P


def layout(lengths, group_rows):
    seq_ends = jnp.cumsum(lengths)
    starts = seq_ends - lengths
    row_index = jnp.arange(group_rows, dtype=jnp.int32)
    seg_ids = jnp.sum((row_index[:, None] >= seq_ends[None, :]).astype(jnp.int32), axis=1)
    owner_mask = seg_ids[:, None] == jnp.arange(lengths.shape[0], dtype=jnp.int32)[None, :]
    positions = row_index - jnp.sum(jnp.where(owner_mask, starts[None, :], 0), axis=1)
    return (seg_ids, positions)


def layer_norm(values, gain_vec, shift_vec):
    average = jnp.mean(values, axis=-1, keepdims=True)
    centred = values - average
    spread = jnp.mean(centred * centred, axis=-1, keepdims=True)
    return centred * lax.rsqrt(spread + 1e-05) * gain_vec + shift_vec


def rotary_tables(positions, head_dim):
    rot_dims = head_dim // 4
    half_rot = rot_dims // 2
    inv_freq = 10000.0 ** (-(jnp.arange(half_rot, dtype=jnp.float32) * 2.0 / rot_dims))
    angles = positions.astype(jnp.float32)[:, None] * inv_freq[None, :]
    angles = jnp.concatenate([angles, angles], axis=-1)
    return (jnp.cos(angles), jnp.sin(angles))


def rotate(vectors, cosine_table, sine_table):
    rot_dims = cosine_table.shape[-1]
    half_rot = rot_dims // 2
    rot_part = vectors[..., :rot_dims]
    turned = jnp.concatenate([-rot_part[..., half_rot:], rot_part[..., :half_rot]], axis=-1)
    result = rot_part * cosine_table[:, None, :] + turned * sine_table[:, None, :]
    return jnp.concatenate([result, vectors[..., rot_dims:]], axis=-1)


def exact_gelu(values):
    return jax.nn.gelu(values, approximate=False)


def body(
    hidden_in,
    out_grad,
    seq_lengths,
    attn_gain,
    attn_shift,
    mlp_gain,
    mlp_shift,
    qkv_weight,
    qkv_bias,
    dense_weight,
    dense_bias,
    fc_weight,
    fc_bias,
    proj_weight,
    proj_bias,
):
    tensor_index = lax.axis_index("tensor")
    tensor_count = lax.axis_size("tensor")
    local_rows = hidden_in.shape[0]
    group_rows = local_rows * tensor_count
    gathered = (
        lax.all_gather(qkv_weight, "dp", axis=0, tiled=True),
        lax.all_gather(dense_weight, "dp", axis=0, tiled=True),
        lax.all_gather(fc_weight, "dp", axis=0, tiled=True),
        lax.all_gather(proj_weight, "dp", axis=0, tiled=True),
        lax.all_gather(attn_gain, "dp", axis=0, tiled=True),
        lax.all_gather(attn_shift, "dp", axis=0, tiled=True),
        lax.all_gather(mlp_gain, "dp", axis=0, tiled=True),
        lax.all_gather(mlp_shift, "dp", axis=0, tiled=True),
        lax.all_gather(qkv_bias, "dp", axis=0, tiled=True),
        lax.all_gather(dense_bias, "dp", axis=0, tiled=True),
        lax.all_gather(fc_bias, "dp", axis=0, tiled=True),
        lax.all_gather(proj_bias, "dp", axis=0, tiled=True),
    )
    (
        w_qkv,
        w_dense,
        w_fc,
        w_proj,
        gain_attn,
        shift_attn,
        gain_mlp,
        shift_mlp,
        bias_qkv,
        bias_dense,
        bias_fc,
        bias_proj,
    ) = gathered
    model_width = w_qkv.shape[0]
    head_count = w_qkv.shape[1]
    triple_width = w_qkv.shape[2]
    head_dim = w_dense.shape[2]
    hidden_units = w_fc.shape[1]
    qkv_cols = head_count * triple_width
    attn_cols = head_count * head_dim
    my_bias_qkv = lax.dynamic_slice_in_dim(bias_qkv, tensor_index * qkv_cols, qkv_cols).astype(
        jnp.float32
    )
    my_bias_fc = lax.dynamic_slice_in_dim(
        bias_fc, tensor_index * hidden_units, hidden_units
    ).astype(jnp.float32)
    gain_attn_f = gain_attn.astype(jnp.float32)
    shift_attn_f = shift_attn.astype(jnp.float32)
    gain_mlp_f = gain_mlp.astype(jnp.float32)
    shift_mlp_f = shift_mlp.astype(jnp.float32)
    seg_ids, positions = layout(seq_lengths[0], group_rows)
    x_rows = hidden_in.astype(jnp.float32)

    def norms(values, gain_one, shift_one, gain_two, shift_two):
        return (layer_norm(values, gain_one, shift_one), layer_norm(values, gain_two, shift_two))

    (normed_one, normed_two), norm_back = jax.vjp(
        norms, x_rows, gain_attn_f, shift_attn_f, gain_mlp_f, shift_mlp_f
    )
    normed_attn, normed_mlp = (
        lax.all_gather(normed_one.astype(jnp.bfloat16), "tensor", axis=0, tiled=True),
        lax.all_gather(normed_two.astype(jnp.bfloat16), "tensor", axis=0, tiled=True),
    )
    merged_lin = (
        jnp.dot(
            normed_attn, w_qkv.reshape(model_width, qkv_cols), preferred_element_type=jnp.float32
        )
        + my_bias_qkv
    )
    merged_lin = merged_lin.reshape(group_rows, head_count, triple_width)
    cosine_table, sine_table = rotary_tables(positions, head_dim)

    def turn_pair(query_lin, key_lin):
        return (
            rotate(query_lin, cosine_table, sine_table),
            rotate(key_lin, cosine_table, sine_table),
        )

    (query_rot, key_rot), turn_back = jax.vjp(
        turn_pair, merged_lin[..., :head_dim], merged_lin[..., head_dim : 2 * head_dim]
    )
    query_low = query_rot.astype(jnp.bfloat16)
    key_low = key_rot.astype(jnp.bfloat16)
    value_low = merged_lin[..., 2 * head_dim :].astype(jnp.bfloat16)
    score_scale = head_dim ** (-0.5)
    block_rows = min(512, group_rows)
    block_count = group_rows // block_rows
    row_index = jnp.arange(group_rows, dtype=jnp.int32)

    def masked_scores(number):
        begin_row = number * block_rows
        end_row = begin_row + block_rows
        scores = (
            jnp.einsum(
                "qhd,khd->hqk",
                query_low[begin_row:end_row],
                key_low[:end_row],
                preferred_element_type=jnp.float32,
            )
            * score_scale
        )
        allowed = (row_index[None, :end_row] <= row_index[begin_row:end_row, None]) & (
            seg_ids[None, :end_row] == seg_ids[begin_row:end_row, None]
        )
        return jnp.where(allowed[None], scores, -1e30)

    head_blocks = []
    log_totals = []
    for number in range(block_count):
        end_row = (number + 1) * block_rows
        scores = masked_scores(number)
        peak_score = jnp.max(scores, axis=-1, keepdims=True)
        weights = jnp.exp(scores - peak_score)
        norm_total = jnp.sum(weights, axis=-1, keepdims=True)
        log_totals.append(peak_score + jnp.log(norm_total))
        prob_low = (weights / norm_total).astype(jnp.bfloat16)
        head_blocks.append(
            jnp.einsum(
                "hqk,khd->qhd", prob_low, value_low[:end_row], preferred_element_type=jnp.float32
            )
        )
    heads_flat = (
        jnp.concatenate(head_blocks, axis=0).astype(jnp.bfloat16).reshape(group_rows, attn_cols)
    )
    attn_part = jnp.einsum(
        "gc,dc->gd",
        heads_flat,
        w_dense.reshape(model_width, attn_cols),
        preferred_element_type=jnp.float32,
    )
    fc_pre = jnp.dot(normed_mlp, w_fc, preferred_element_type=jnp.float32) + my_bias_fc
    act_full, gelu_back = jax.vjp(exact_gelu, fc_pre)
    act_low = act_full.astype(jnp.bfloat16)
    mlp_part = jnp.einsum("gf,df->gd", act_low, w_proj, preferred_element_type=jnp.float32)
    branch_rows = lax.psum_scatter(
        (attn_part + mlp_part).astype(jnp.bfloat16), "tensor", scatter_dimension=0, tiled=True
    ).astype(jnp.float32)
    block_out = (
        x_rows + branch_rows + bias_dense.astype(jnp.float32) + bias_proj.astype(jnp.float32)
    ).astype(jnp.bfloat16)
    w_qkv, w_dense, w_fc, w_proj = (
        lax.all_gather(qkv_weight, "dp", axis=0, tiled=True),
        lax.all_gather(dense_weight, "dp", axis=0, tiled=True),
        lax.all_gather(fc_weight, "dp", axis=0, tiled=True),
        lax.all_gather(proj_weight, "dp", axis=0, tiled=True),
    )
    cot_all = lax.all_gather(out_grad, "tensor", axis=0, tiled=True)
    grad_act = jnp.dot(cot_all, w_proj, preferred_element_type=jnp.float32)
    grad_proj = jnp.einsum("gd,gf->df", cot_all, act_low, preferred_element_type=jnp.float32)
    grad_pre = gelu_back(grad_act)[0].astype(jnp.bfloat16)
    grad_fc = jnp.einsum("gd,gf->df", normed_mlp, grad_pre, preferred_element_type=jnp.float32)
    fc_bias_part = jnp.sum(grad_pre, axis=0, dtype=jnp.float32)
    grad_normed_mlp = jnp.einsum("gf,df->gd", grad_pre, w_fc, preferred_element_type=jnp.float32)
    dense_flat = w_dense.reshape(model_width, attn_cols)
    grad_heads = (
        jnp.dot(cot_all, dense_flat, preferred_element_type=jnp.float32)
        .astype(jnp.bfloat16)
        .reshape(group_rows, head_count, head_dim)
    )
    grad_dense = jnp.einsum(
        "gd,gc->dc", cot_all, heads_flat, preferred_element_type=jnp.float32
    ).reshape(model_width, head_count, head_dim)
    query_grads = []
    grad_key = jnp.zeros((group_rows, head_count, head_dim), jnp.float32)
    grad_value = jnp.zeros((group_rows, head_count, head_dim), jnp.float32)
    for number in range(block_count):
        begin_row = number * block_rows
        end_row = begin_row + block_rows
        probs = jnp.exp(masked_scores(number) - log_totals[number])
        heads_blk = grad_heads[begin_row:end_row]
        grad_probs = jnp.einsum(
            "qhd,khd->hqk", heads_blk, value_low[:end_row], preferred_element_type=jnp.float32
        )
        row_delta = jnp.sum(probs * grad_probs, axis=-1, keepdims=True)
        grad_scores = (probs * (grad_probs - row_delta)).astype(jnp.bfloat16)
        query_grads.append(
            jnp.einsum(
                "hqk,khd->qhd", grad_scores, key_low[:end_row], preferred_element_type=jnp.float32
            )
            * score_scale
        )
        grad_key = grad_key.at[:end_row].add(
            jnp.einsum(
                "hqk,qhd->khd",
                grad_scores,
                query_low[begin_row:end_row],
                preferred_element_type=jnp.float32,
            )
            * score_scale
        )
        grad_value = grad_value.at[:end_row].add(
            jnp.einsum(
                "hqk,qhd->khd",
                probs.astype(jnp.bfloat16),
                heads_blk,
                preferred_element_type=jnp.float32,
            )
        )
    grad_query = jnp.concatenate(query_grads, axis=0)
    grad_query_lin, grad_key_lin = turn_back((grad_query, grad_key))
    grad_merged = (
        jnp.concatenate([grad_query_lin, grad_key_lin, grad_value], axis=-1)
        .astype(jnp.bfloat16)
        .reshape(group_rows, qkv_cols)
    )
    grad_qkv = jnp.einsum(
        "gd,gc->dc", normed_attn, grad_merged, preferred_element_type=jnp.float32
    ).reshape(model_width, head_count, triple_width)
    qkv_bias_part = jnp.sum(grad_merged, axis=0, dtype=jnp.float32)
    grad_normed_attn = jnp.einsum(
        "gc,dc->gd",
        grad_merged,
        w_qkv.reshape(model_width, qkv_cols),
        preferred_element_type=jnp.float32,
    )
    cot_rows = out_grad.astype(jnp.float32)
    local_attn, local_mlp = (
        lax.psum_scatter(
            grad_normed_attn.astype(jnp.bfloat16), "tensor", scatter_dimension=0, tiled=True
        ).astype(jnp.float32),
        lax.psum_scatter(
            grad_normed_mlp.astype(jnp.bfloat16), "tensor", scatter_dimension=0, tiled=True
        ).astype(jnp.float32),
    )
    grad_x, grad_gain_attn, grad_shift_attn, grad_gain_mlp, grad_shift_mlp = norm_back(
        (local_attn, local_mlp)
    )
    input_grad = cot_rows + grad_x
    cot_sums = jnp.sum(cot_rows, axis=0)
    full_qkv_bias = lax.dynamic_update_slice_in_dim(
        jnp.zeros((qkv_cols * tensor_count,), jnp.float32),
        qkv_bias_part,
        tensor_index * qkv_cols,
        0,
    )
    full_fc_bias = lax.dynamic_update_slice_in_dim(
        jnp.zeros((hidden_units * tensor_count,), jnp.float32),
        fc_bias_part,
        tensor_index * hidden_units,
        0,
    )
    small_sums = (
        lax.psum_scatter(grad_gain_attn, ("dp", "tensor"), scatter_dimension=0, tiled=True),
        lax.psum_scatter(grad_shift_attn, ("dp", "tensor"), scatter_dimension=0, tiled=True),
        lax.psum_scatter(grad_gain_mlp, ("dp", "tensor"), scatter_dimension=0, tiled=True),
        lax.psum_scatter(grad_shift_mlp, ("dp", "tensor"), scatter_dimension=0, tiled=True),
        lax.psum_scatter(full_qkv_bias, ("dp", "tensor"), scatter_dimension=0, tiled=True),
        lax.psum_scatter(cot_sums, ("dp", "tensor"), scatter_dimension=0, tiled=True),
        lax.psum_scatter(full_fc_bias, ("dp", "tensor"), scatter_dimension=0, tiled=True),
    )
    large_sums = (
        lax.psum_scatter(grad_qkv, "dp", scatter_dimension=0, tiled=True),
        lax.psum_scatter(grad_dense, "dp", scatter_dimension=0, tiled=True),
        lax.psum_scatter(grad_fc, "dp", scatter_dimension=0, tiled=True),
        lax.psum_scatter(grad_proj, "dp", scatter_dimension=0, tiled=True),
    )
    return (
        block_out,
        input_grad,
        small_sums[0],
        small_sums[1],
        small_sums[2],
        small_sums[3],
        large_sums[0],
        small_sums[4],
        large_sums[1],
        small_sums[5],
        large_sums[2],
        small_sums[6],
        large_sums[3],
        small_sums[5],
    )


def solution(mesh):
    in_specs = (
        P(("dp", "tensor"), None),
        P(("dp", "tensor"), None),
        P("dp", None),
        P("dp"),
        P("dp"),
        P("dp"),
        P("dp"),
        P("dp", "tensor", None),
        P("dp"),
        P("dp", "tensor", None),
        P("dp"),
        P("dp", "tensor"),
        P("dp"),
        P("dp", "tensor"),
        P("dp"),
    )
    out_specs = (
        P(("dp", "tensor"), None),
        P(("dp", "tensor"), None),
        P(("dp", "tensor")),
        P(("dp", "tensor")),
        P(("dp", "tensor")),
        P(("dp", "tensor")),
        P("dp", "tensor", None),
        P(("dp", "tensor")),
        P("dp", "tensor", None),
        P(("dp", "tensor")),
        P("dp", "tensor"),
        P(("dp", "tensor")),
        P("dp", "tensor"),
        P(("dp", "tensor")),
    )
    return jax.shard_map(body, mesh=mesh, in_specs=in_specs, out_specs=out_specs, check_vma=False)
```

profile of v0, /device:TPU:0, one launch (start us, length us, event | category | flops | bytes accessed | tf_op | source)
XLA Modules:
  0.0 1064.3 jit_solution(6079659336549797893)
XLA Ops:
  18.7 79.0 %all-reduce.26 = (bf16[768]{0:T(1024)(128)(2,1)S(1)}, bf16[768]{0:T(1024)(128)(2,1)S(1)}, bf16[3072]{0:T(1024)(128)(2,1)S(1)}, bf16[768]{0:T(1024)(128)(2,1)S(1)...) all-reduce(bf16[768]{0:T(1024)(128)(2,1)S(1)} %dynamic-update-slice, ...), channel_id=1, replica_groups=mesh['dp'=16,'tensor'=2] {'dp'}, use_global_device_ids=true, to_apply=%add.14 | all-reduce | flops 9984 | bytes 39936
  97.7 1.7 convert_reduce_fusion.4
  100.6 2.6 fusion.41
  105.9 44.1 %all_gather.54 = bf16[768,6,64]{2,0,1:T(8,128)(2,1)S(1)} all-gather(bf16[48,6,64]{2,0,1:T(8,128)(2,1)S(1)} %copy-done.50), channel_id=1, replica_groups=mesh['dp'=16,'tensor'=2] {'dp'}, dimensions={0}, use_global_device_ids=true | all-gather | bytes 626688 | tf_op jit(solution)/shard_map/all_gather | solution.py:69
  152.3 2.0 fusion.37
  155.6 1.6 compare_and_fusion
  157.1 3.3 convolution_convert_fusion.1
  161.7 3.3 copy.54
  165.0 5.8 convolution_add_fusion
  176.1 2.0 fusion.95
  178.1 4.0 multiply_reduce_fusion.3
  182.0 4.6 multiply_convert_fusion.4
  186.7 1.5 fusion.102
  189.3 2.6 fusion.152
  191.9 2.6 fusion.14
  194.6 6.1 multiply_reduce_fusion.2
  200.7 6.3 multiply_convert_fusion.2
  206.9 3.0 fusion.101
  211.7 8.4 fusion.153
  220.1 9.0 fusion.2
  229.1 12.9 %multiply_reduce_fusion.1 = (f32[6,512]{1,0:T(8,128)S(1)}, f32[6,512,1536]{2,1,0:T(8,128)}) fusion(f32[6,512,1536]{2,1,0:T(8,128)} %get-tuple-element.251, f32[6,512]{1,0:T(8,128)S(1)} %log_add_fusion.1, bf16[512,6,64]{0,2,1:T(8,128)(2,1)} %bitcast.138, bf16[2048,6,192]{0,2,1:T(8,128)(2,1)} %copy-done.9), kind=kOutput, calls=%fused_computation.10 | convolution fusion | flops 618132480 | bytes 39346176 | tf_op jit(solution)/shard_map/qhd,khd->hqk/dot_general | solution.py:232
  242.1 13.0 %multiply_convert_fusion.1 = bf16[6,512,1536]{2,1,0:T(8,128)(2,1)S(1)} fusion(f32[6,512,1536]{2,1,0:T(8,128)} %get-tuple-element.257, f32[6,512,1536]{2,1,0:T(8,128)} %get-tuple-element.251, f32[6,512]{1,0:T(8,128)S(1)} %get-tuple-element.256, f32[6,512]{1,0:T(8,128)S(1)} %log_add_fusion.1), kind=kLoop, calls=%fused_computation.9 | loop fusion | flops 18874368 | bytes 47210496 | tf_op jit(solution)/shard_map/convert_element_type | solution.py:236
  255.1 3.8 fusion.100
  258.9 1.8 fusion.61
  260.8 10.7 %fusion.154 = (f32[6,512]{1,0:T(8,128)S(1)}, f32[6,512,2048]{2,1,0:T(8,128)}) fusion(bf16[512,6,64]{0,2,1:T(8,128)(2,1)S(1)} %copy-done.32, bf16[2048,6,16]{0,2,1:T(8,128)(2,1)S(1)} %get-tuple-element.213, bf16[2048,6,48]{0,2,1:T(8,128)(2,1)S(1)} %get-tuple-element.219, pred[512,2048]{1,0:T(8,128)(4,1)S(1)} %copy-done.38), kind=kOutput, calls=%fused_computation.253 | convolution fusion | flops 827323392 | bytes 28192768 | tf_op jit(solution)/shard_map/qhd,khd->hqk/dot_general | solution.py:155
  271.5 10.5 fusion
  282.0 16.2 %multiply_reduce_fusion = (f32[6,512]{1,0:T(8,128)S(1)}, f32[6,512,2048]{2,1,0:T(8,128)}) fusion(f32[6,512,2048]{2,1,0:T(8,128)} %get-tuple-element.253, f32[6,512]{1,0:T(8,128)S(1)} %log_add_fusion, bf16[512,6,64]{0,2,1:T(8,128)(2,1)S(1)} %bitcast.136, bf16[2048,6,192]{0,2,1:T(8,128)(2,1)} %copy-done.9), kind=kOutput, calls=%fused_computation.1 | convolution fusion | flops 824177664 | bytes 52322304 | tf_op jit(solution)/shard_map/qhd,khd->hqk/dot_general | solution.py:232
  298.2 17.0 %multiply_convert_fusion = bf16[6,512,2048]{2,1,0:T(8,128)(2,1)S(1)} fusion(f32[6,512,2048]{2,1,0:T(8,128)} %get-tuple-element.255, f32[6,512,2048]{2,1,0:T(8,128)} %get-tuple-element.253, f32[6,512]{1,0:T(8,128)S(1)} %get-tuple-element.254, f32[6,512]{1,0:T(8,128)S(1)} %log_add_fusion), kind=kLoop, calls=%fused_computation | loop fusion | flops 25165824 | bytes 62939136 | tf_op jit(solution)/shard_map/convert_element_type | solution.py:236
  315.2 4.4 copy-done.2
  319.7 6.1 fusion.99
  325.8 8.0 bitcast_add_fusion.2
  333.9 5.1 pad_maximum_fusion
  339.1 1.6 broadcast_multiply_fusion
  341.8 2.1 scatter-add.25
  344.8 4.5 fusion.88
  349.4 6.4 fusion.68
  355.8 11.6 %bitcast_add_fusion.1 = bf16[2048,6,64]{0,2,1:T(8,128)(2,1)S(1)} fusion(f32[2048,6,64]{0,2,1:T(8,128)} %fusion.68, bf16[512,6,64]{0,2,1:T(8,128)(2,1)S(1)} %bitcast.137, f32[6,512,2048]{2,1,0:T(8,128)} %get-tuple-element.253, f32[6,512]{1,0:T(8,128)S(1)} %log_add_fusion), kind=kOutput, calls=%fused_computation.109 | convolution fusion | flops 819462144 | bytes 30289920 | tf_op jit(solution)/shard_map/hqk,qhd->khd/dot_general | solution.py:253
  372.0 1.7 convert_reduce_fusion.1
  373.7 2.1 copy-done.20
  375.9 6.6 bitcast_convert_fusion
  382.5 9.3 fusion.105
  392.5 34.9 %multiply_convert_fusion.3 = (bf16[2048,1536]{1,0:T(8,128)(2,1)}, f32[2048,1536]{1,0:T(8,128)}, f32[2048,1536]{1,0:T(8,128)}) fusion(f32[1536]{0:T(1024)S(1)} %copy-done.64, bf16[2048,768]{1,0:T(8,128)(2,1)} %all-gather.11.cloned.1.call-done, bf16[768,1536]{1,0:T(8,128)(2,1)} %all-gather.13.cloned.1.call-done), kind=kOutput, calls=%fused_computation.25 | convolution fusion | flops 5039456256 | bytes 36968448 | tf_op jit(solution)/shard_map/dot_general | solution.py:192
  427.3 17.0 %convert_reduce_fusion = (f32[1536]{0:T(1024)S(1)}, bf16[2048,1536]{1,0:T(8,128)(2,1)S(1)}) fusion(f32[2048,1536]{1,0:T(8,128)} %get-tuple-element.212, bf16[2048,768]{1,0:T(8,128)(2,1)} %all-gather.17.cloned.1.call-done, bf16[768,1536]{1,0:T(8,128)(2,1)} %all-gather.15.cloned.1.call-done, f32[2048,1536]{1,0:T(8,128)} %get-tuple-element.245, ...), kind=kOutput, calls=%fused_computation.19 | convolution fusion | flops 4885314048 | bytes 36974592 | tf_op jit(solution)/shard_map/dot_general | solution.py:209
  444.3 2.6 copy-done.72
  446.9 6.4 convolution_convert_fusion
  454.0 7.7 fusion.104
  461.8 4.1 fusion.103
  466.0 11.1 %fusion.106 = bf16[6,64,512]{2,1,0:T(8,128)(2,1)S(1)} fusion(f32[6,512,2048]{2,1,0:T(8,128)} %get-tuple-element.253, f32[6,512]{1,0:T(8,128)S(1)} %copy-done.60, f32[6,512]{1,0:T(8,128)S(1)} %copy-done.58, bf16[2048,6,192]{0,2,1:T(8,128)(2,1)} %copy-done.9), kind=kOutput, calls=%fused_computation.174 | convolution fusion | flops 824377344 | bytes 27156480 | tf_op jit(solution)/shard_map/hqk,khd->qhd/dot_general | solution.py:179
  477.1 7.3 fusion.155
  484.5 4.6 fusion.22
  489.1 3.3 fusion.80
  492.4 1.9 copy.61
  494.4 10.0 fusion.33
  504.5 9.8 fusion.156
  514.4 9.7 convolution_bitcast_fusion
  524.1 6.2 copy.69
  531.7 3.9 fusion.45
  535.6 3.3 fusion.50
  539.0 6.5 convert_reduce_fusion.5
  545.5 37.6 %all-reduce.25 = (f32[768]{0:T(1024)S(1)}, f32[768]{0:T(1024)S(1)}, f32[768]{0:T(1024)S(1)}, f32[768]{0:T(1024)S(1)}, f32[2304]{0:T(1024)S(1)}, /*index=5*/f32[768]{0:T(1024)S(1)}, f32[3072]{0:T(1024)S(1)}) all-reduce(f32[768]{0:T(1024)S(1)} %get-tuple-element.187, ...), channel_id=5, replica_groups=mesh['dp'=16,'tensor'=2] {'dp','tensor'}, use_global_device_ids=true, to_apply=%region_25.26.clone | all-reduce | flops 9216 | bytes 73728
  586.7 45.2 %reduce-scatter.18.cloned.1.call-done = f32[48,6,64]{2,0,1:T(8,128)} async-done(((f32[768,6,64]{2,0,1:T(8,128)}), f32[48,6,64]{2,0,1:T(8,128)}) %reduce-scatter.18.cloned.1.call-update) | async-done | bytes 73744 | tf_op jit(solution)/shard_map/reduce_scatter | solution.py:314
  631.9 141.2 %reduce-scatter.16.cloned.1.call-done = f32[48,6,192]{2,0,1:T(8,128)} async-done(((f32[768,6,192]{2,0,1:T(8,128)}), f32[48,6,192]{2,0,1:T(8,128)}) %reduce-scatter.16.cloned.1.call-update) | async-done | bytes 221200 | tf_op jit(solution)/shard_map/reduce_scatter | solution.py:313
  773.2 142.5 %reduce-scatter.20.cloned.1.call-done = f32[48,1536]{1,0:T(8,128)} async-done(((f32[768,1536]{1,0:T(8,128)}), f32[48,1536]{1,0:T(8,128)}) %reduce-scatter.20.cloned.1.call-update) | async-done | bytes 294928 | tf_op jit(solution)/shard_map/reduce_scatter | solution.py:315
  915.7 141.4 %reduce-scatter.22.cloned.1.call-done = f32[48,1536]{1,0:T(8,128)} async-done(((f32[768,1536]{1,0:T(8,128)}), f32[48,1536]{1,0:T(8,128)}) %reduce-scatter.22.cloned.1.call-update) | async-done | bytes 294928
  (282 shorter events, 40.0 us)
Async XLA Ops:
  7.2 92.2 %copy-start.3 = (bf16[1024,768]{1,0:T(8,128)(2,1)S(1)}, bf16[1024,768]{1,0:T(8,128)(2,1)}, u32[]{:S(2)}) copy-start(bf16[1024,768]{1,0:T(8,128)(2,1)} %param.35) | copy-start | bytes 4718596
  7.2 149.9 %all-gather.17.cloned.1.call-start = ((), (), s32[]{:S(2)}) async-start(), calls=%async_computation.13 | async-start | bytes 4718592 | tf_op jit(solution)/shard_map/all_gather | solution.py:208
  7.9 153.8 %all-gather.9.cloned.1.call-start = ((), (), s32[]{:S(2)}) async-start(), calls=%async_computation.8 | async-start | bytes 2506752 | tf_op jit(solution)/shard_map/all_gather | solution.py:68
  8.7 156.3 %all-gather.7.cloned.1.call-start = ((), (), s32[]{:S(2)}) async-start(), calls=%async_computation.7 | async-start | bytes 4718592 | tf_op jit(solution)/shard_map/all_gather | solution.py:122
  97.7 5.5 copy-start.46
  97.7 5.5 copy-start.48
  99.4 3.8 copy-start.40
  100.6 4.5 copy-start.69
  103.2 288.6 %all-gather.11.cloned.1.call-start = ((), (), s32[]{:S(2)}) async-start(), calls=%async_computation.9 | async-start | bytes 4718592 | tf_op jit(solution)/shard_map/all_gather | solution.py:123
  103.8 288.1 %all-gather.13.cloned.1.call-start = ((), (), s32[]{:S(2)}) async-start(), calls=%async_computation.10 | async-start | bytes 2506752 | tf_op jit(solution)/shard_map/all_gather | solution.py:70
  104.4 322.9 %all-gather.15.cloned.1.call-start = ((), (), s32[]{:S(2)}) async-start(), calls=%async_computation.11 | async-start | bytes 2506752 | tf_op jit(solution)/shard_map/all_gather | solution.py:71
  105.0 426.6 %reduce-scatter.14.cloned.1.call-start = ((), (), s32[]{:S(2)}) async-start(), calls=%async_computation.15 | async-start | bytes 4718592 | tf_op jit(solution)/shard_map/reduce_scatter | solution.py:279
  105.9 66.1 %copy-start.33 = (f32[2048,16]{0,1:T(8,128)}, f32[2048,16]{0,1:T(8,128)S(1)}, u32[]{:S(2)}) copy-start(f32[2048,16]{0,1:T(8,128)S(1)} %get-tuple-element.237) | copy-start | bytes 393220
  105.9 66.1 %copy-start.35 = (f32[2048,16]{0,1:T(8,128)}, f32[2048,16]{0,1:T(8,128)S(1)}, u32[]{:S(2)}) copy-start(f32[2048,16]{0,1:T(8,128)S(1)} %get-tuple-element.238) | copy-start | bytes 393220
  150.0 10.5 copy-start.18
  171.7 22.8 %copy-start.9 = (bf16[2048,6,192]{0,2,1:T(8,128)(2,1)}, bf16[2048,6,192]{0,2,1:T(8,128)(2,1)S(1)}, u32[]{:S(2)}) copy-start(bf16[2048,6,192]{0,2,1:T(8,128)(2,1)S(1)} %convert.33) | copy-start | bytes 14155780
  171.9 88.8 %copy-start.5 = (bf16[2048,6,48]{0,2,1:T(8,128)(2,1)}, bf16[2048,6,48]{0,2,1:T(8,128)(2,1)S(1)}, u32[]{:S(2)}) copy-start(bf16[2048,6,48]{0,2,1:T(8,128)(2,1)S(1)} %get-tuple-element.219) | copy-start | bytes 3538948
  174.8 7.2 copy-start.1
  191.9 8.8 copy-start
  194.5 6.1 copy-start.55
  211.7 8.4 copy-start.6
  255.1 3.8 copy-start.7
  260.7 10.8 %copy-start.8 = (f32[2048,6,64]{0,2,1:T(8,128)}, f32[2048,6,64]{0,2,1:T(8,128)S(1)}, u32[]{:S(2)}) copy-start(f32[2048,6,64]{0,2,1:T(8,128)S(1)} %fusion.61) | copy-start | bytes 9437188
  271.5 10.5 copy-start.57
  271.5 10.5 copy-start.21
  282.0 16.2 %copy-start.59 = (f32[6,512]{1,0:T(8,128)}, f32[6,512]{1,0:T(8,128)S(1)}, u32[]{:S(2)}) copy-start(f32[6,512]{1,0:T(8,128)S(1)} %fusion) | copy-start | bytes 36868
  315.2 4.5 copy-start.2
  325.8 8.1 copy-start.14
  325.8 8.1 copy-start.15
  325.8 8.1 copy-start.16
  325.8 18.1 %slice-start = ((s8[12582912]{0:T(1024)(128)(4,1)}), s8[4194304]{0:T(1024)(128)(4,1)S(1)}, s32[]{:S(2)}) async-start(s8[12582912]{0:T(1024)(128)(4,1)} %bitcast.129), calls=%async_computation.20 | async-start | bytes 8388608
  325.8 18.1 %slice-start.1 = ((s8[12582912]{0:T(1024)(128)(4,1)}), s8[4194304]{0:T(1024)(128)(4,1)S(1)}, s32[]{:S(2)}) async-start(s8[12582912]{0:T(1024)(128)(4,1)} %bitcast.129), calls=%async_computation.21 | async-start | bytes 8388608
  325.8 23.6 %slice-start.3 = ((s8[18874368]{0:T(1024)(128)(4,1)}), s8[4194304]{0:T(1024)(128)(4,1)S(1)}, s32[]{:S(2)}) async-start(s8[18874368]{0:T(1024)(128)(4,1)} %bitcast.131), calls=%async_computation.23 | async-start | bytes 8388608
  325.8 23.6 %slice-start.4 = ((s8[18874368]{0:T(1024)(128)(4,1)}), s8[4194304]{0:T(1024)(128)(4,1)S(1)}, s32[]{:S(2)}) async-start(s8[18874368]{0:T(1024)(128)(4,1)} %bitcast.131), calls=%async_computation.24 | async-start | bytes 8388608
  333.9 5.2 copy-start.10
  333.9 5.2 copy-start.17
  333.9 5.2 copy-start.36
  333.9 15.5 %slice-start.5 = ((s8[18874368]{0:T(1024)(128)(4,1)}), s8[4194304]{0:T(1024)(128)(4,1)S(1)}, s32[]{:S(2)}) async-start(s8[18874368]{0:T(1024)(128)(4,1)} %bitcast.131), calls=%async_computation.25 | async-start | bytes 8388608
  339.1 4.8 slice-start.2
  340.7 8.7 slice-start.6
  341.8 3.1 copy-start.25
  344.8 4.6 slice-start.7
  349.4 6.4 copy-start.22
  355.8 11.6 %copy-start.28 = (f32[2048,6,16]{0,2,1:T(8,128)S(1)}, f32[2048,6,16]{0,2,1:T(8,128)}, u32[]{:S(2)}) copy-start(f32[2048,6,16]{0,2,1:T(8,128)} %get-tuple-element.209) | copy-start | bytes 2359300
  372.0 3.8 copy-start.30
  391.8 139.8 %reduce-scatter.12.cloned.1.call-start = ((), (), s32[]{:S(2)}) async-start(), calls=%async_computation.14 | async-start | bytes 4718592 | tf_op jit(solution)/shard_map/reduce_scatter | solution.py:282
  427.3 19.6 %copy-start.68 = (bf16[768,1536]{1,0:T(8,128)(2,1)S(1)}, bf16[768,1536]{1,0:T(8,128)(2,1)}, u32[]{:S(2)}) copy-start(bf16[768,1536]{1,0:T(8,128)(2,1)} %all-gather.13.cloned.1.call-done) | copy-start | bytes 7077892
  453.3 8.4 copy-start.43
  453.4 8.4 copy-start.54
  453.4 85.6 %reduce-scatter.10.cloned.1.call-start = ((), (), s32[]{:S(2)}) async-start(), calls=%async_computation.12 | async-start | bytes 4718592 | tf_op jit(solution)/shard_map/reduce_scatter | solution.py:196
  461.8 4.2 copy-start.58
  461.8 4.2 copy-start.60
  466.0 11.1 %copy-start.67 = (bf16[768,1536]{1,0:T(8,128)(2,1)S(1)}, bf16[768,1536]{1,0:T(8,128)(2,1)}, u32[]{:S(2)}) copy-start(bf16[768,1536]{1,0:T(8,128)(2,1)} %all-gather.15.cloned.1.call-done) | copy-start | bytes 7077892
  477.1 7.3 copy-start.19
  477.1 7.3 copy-start.70
  489.1 142.9 %reduce-scatter.18.cloned.1.call-start = ((), (), s32[]{:S(2)}) async-start(), calls=%async_computation.17 | async-start | bytes 2506752 | tf_op jit(solution)/shard_map/reduce_scatter | solution.py:314
  494.3 278.8 %reduce-scatter.16.cloned.1.call-start = ((), (), s32[]{:S(2)}) async-start(), calls=%async_computation.16 | async-start | bytes 5013504 | tf_op jit(solution)/shard_map/reduce_scatter | solution.py:313
  504.4 411.2 %reduce-scatter.20.cloned.1.call-start = ((), (), s32[]{:S(2)}) async-start(), calls=%async_computation.18 | async-start | bytes 5013504 | tf_op jit(solution)/shard_map/reduce_scatter | solution.py:315
  514.3 542.7 %reduce-scatter.22.cloned.1.call-start = ((), (), s32[]{:S(2)}) async-start(), calls=%async_computation.19 | async-start | bytes 5013504
  530.3 5.3 copy-start.62
  530.3 5.3 copy-start.52
  531.6 4.0 copy-start.12
  531.7 3.9 copy-start.13
  583.8 473.7 %copy-start.71 = (f32[24]{0:T(128)}, f32[24]{0:T(128)S(1)}, u32[]{:S(2)}) copy-start(f32[24]{0:T(128)S(1)} %dynamic-slice.72) | copy-start | bytes 292
  (32 other events, 52.8 us)
Sparse Core Ops, SparseCore 0:
  9.6 14.8 all-gather.16
  27.1 64.0 all-gather.8
  103.4 7.9 all-gather.6
  112.8 13.2 all-gather.10
  128.8 63.9 all-gather.12
  195.5 61.1 all-gather.14
  391.9 8.4 reduce-scatter.13
  453.5 8.4 reduce-scatter.11
  489.2 7.8 reduce-scatter.9
  503.2 128.6 reduce-scatter.17
  637.7 135.4 reduce-scatter.15
  779.6 136.0 reduce-scatter.19
  921.4 135.5 reduce-scatter.21
where the time goes:
time: 1070 us; the launch traced here: 1060 us
  waiting for transfers between devices  473 us (44%)
  matrix products  264 us (25%)
  blocking collectives  161 us (15%)
  other arithmetic  102 us (10%)
  local copies, waits for them, and re-layouts  46.6 us (4%)
  between operations  17.3 us (2%)
    unnamed x14, waiting for transfers between devices  144 us
    reduce_scatter x1, waiting for transfers between devices, body(): lax.psum_scatter(grad_fc, 'dp', scatter_dimension=0, tiled=True)  142 us
    reduce_scatter x1, waiting for transfers between devices, body(): lax.psum_scatter(grad_qkv, 'dp', scatter_dimension=0, tiled=True)  141 us
    unnamed x2, blocking collectives  117 us
    reduce_scatter x1, waiting for transfers between devices, body(): lax.psum_scatter(grad_dense, 'dp', scatter_dimension=0, tiled=True)  45.2 us
    all_gather x1, blocking collectives, body(): lax.all_gather(dense_weight, 'dp', axis=0, tiled=True)  44.1 us
    convert_element_type x4, other arithmetic, body(): grad_scores = (probs * (grad_probs - row_delta)).astype(jnp.bfloat16)  40.9 us
    dot_general x4, matrix products, body(): jnp.einsum('qhd,khd->hqk', heads_blk, value_low[:end_row], preferred_elem...  39.2 us
  transfers between devices with their start and end apart: 13, of which 4 were waited for; matrix products, arithmetic and copies ran while one was open for 37% of the time, Pallas kernels for 0%

commit v1 on v0

--- a/solution.py
+++ b/solution.py
@@ -2,6 +2,27 @@
 import jax.numpy as jnp
 from jax import lax
 from jax.sharding import PartitionSpec as P
+
+
+def note_the_roots(own_rows, axis_no):
+    parts_out = list(own_rows.shape[1:])
+    parts_out[axis_no] *= own_rows.shape[0]
+    row_out = jnp.moveaxis(own_rows, 0, axis_no).reshape(parts_out)
+    return row_out
+
+
+def remake_points(join_dim, chip_axis, q_in):
+    how_many = lax.axis_size(chip_axis)
+    heap = list(map(lambda at: (at, (at + 1) % how_many), range(how_many)))
+    runs = [q_in]
+    while len(runs) < how_many:
+        s_next = lax.ppermute(runs[-1], chip_axis, heap)
+        runs.append(s_next)
+    f_next = lax.axis_index(chip_axis)
+    mid_arr = jnp.stack(runs, axis=0)
+    runs = mid_arr[(f_next - jnp.arange(how_many)) % how_many]
+    arr_next = note_the_roots(runs, join_dim)
+    return arr_next
 
 
 def layout(lengths, group_rows):
@@ -66,7 +87,7 @@
     group_rows = local_rows * tensor_count
     gathered = (
         lax.all_gather(qkv_weight, "dp", axis=0, tiled=True),
-        lax.all_gather(dense_weight, "dp", axis=0, tiled=True),
+        remake_points(0, "dp", dense_weight),
         lax.all_gather(fc_weight, "dp", axis=0, tiled=True),
         lax.all_gather(proj_weight, "dp", axis=0, tiled=True),
         lax.all_gather(attn_gain, "dp", axis=0, tiled=True),

time: 1070 us -> 1210 us (1.13)
  waiting for transfers between devices: 473 us -> 593 us
    ppermute x0 -> x15, waiting for transfers between devices: none -> 120 us  [remake_points(): s_next = lax.ppermute(runs[-1], chip_axis, heap)]
    unnamed x188 -> x201, local copies, waits for them, and re-layouts: 34.7 us -> 35 us
  transfers between devices with their start and end apart: 13 -> 28, of which waited for: 4 -> 18; matrix products, arithmetic and copies ran while one was open for 37% -> 33% of each run, Pallas kernels for 0% -> 0%
where the time goes in v1:
time: 1210 us; the launch traced here: 1200 us
  waiting for transfers between devices  593 us (49%)
  matrix products  264 us (22%)
  blocking collectives  165 us (14%)
  other arithmetic  101 us (8%)
  local copies, waits for them, and re-layouts  49.9 us (4%)
  between operations  17.4 us (1%)
    unnamed x14, waiting for transfers between devices  145 us
    reduce_scatter x1, waiting for transfers between devices, body(): lax.psum_scatter(grad_fc, 'dp', scatter_dimension=0, tiled=True)  142 us
    reduce_scatter x1, waiting for transfers between devices, body(): lax.psum_scatter(grad_qkv, 'dp', scatter_dimension=0, tiled=True)  142 us
    ppermute x15, waiting for transfers between devices, remake_points(): s_next = lax.ppermute(runs[-1], chip_axis, heap)  120 us
    unnamed x2, blocking collectives  117 us
    all_gather x1, blocking collectives, body(): lax.all_gather(dense_weight, 'dp', axis=0, tiled=True)  48.5 us
    reduce_scatter x1, waiting for transfers between devices, body(): lax.psum_scatter(grad_dense, 'dp', scatter_dimension=0, tiled=True)  44.1 us
    convert_element_type x4, other arithmetic, body(): grad_scores = (probs * (grad_probs - row_delta)).astype(jnp.bfloat16)  40.6 us
  transfers between devices with their start and end apart: 28, of which 18 were waited for; matrix products, arithmetic and copies ran while one was open for 33% of the time, Pallas kernels for 0%

profile of v1, /device:TPU:0, one launch (start us, length us, event | category | flops | bytes accessed | tf_op | source)
XLA Modules:
  0.0 1201.7 jit_solution(13932656510108510592)
XLA Ops:
  18.7 79.1 %all-reduce.26 = (bf16[768]{0:T(1024)(128)(2,1)S(1)}, bf16[768]{0:T(1024)(128)(2,1)S(1)}, bf16[3072]{0:T(1024)(128)(2,1)S(1)}, bf16[768]{0:T(1024)(128)(2,1)S(1)...) all-reduce(bf16[768]{0:T(1024)(128)(2,1)S(1)} %dynamic-update-slice, ...), channel_id=1, replica_groups=mesh['dp'=16,'tensor'=2] {'dp'}, use_global_device_ids=true, to_apply=%add.14 | all-reduce | flops 9984 | bytes 39936
  105.5 48.5 %all_gather.62 = bf16[768,6,64]{2,0,1:T(8,128)(2,1)S(1)} all-gather(bf16[48,6,64]{2,0,1:T(8,128)(2,1)S(1)} %copy-done.40), channel_id=1, replica_groups=mesh['dp'=16,'tensor'=2] {'dp'}, dimensions={0}, use_global_device_ids=true | all-gather | bytes 626688 | tf_op jit(solution)/shard_map/all_gather | solution.py:225
  162.4 9.5 collective-permute-done.1
  172.0 8.1 collective-permute-done.2
  180.1 9.0 collective-permute-done.3
  189.1 9.5 collective-permute-done.4
  198.6 7.9 collective-permute-done.5
  206.5 8.9 collective-permute-done.6
  215.4 8.5 collective-permute-done.7
  223.9 9.5 collective-permute-done.8
  233.5 7.9 collective-permute-done.9
  241.4 8.1 collective-permute-done.10
  249.5 9.1 collective-permute-done.11
  258.6 7.9 collective-permute-done.12
  266.6 7.9 collective-permute-done.13
  274.5 10.1 collective-permute-start.14
  284.7 7.9 collective-permute-done.14
  295.5 3.4 convolution_convert_fusion.1
  303.0 5.8 convolution_add_fusion
  316.0 4.0 multiply_reduce_fusion.3
  320.0 4.6 multiply_convert_fusion.4
  327.1 2.8 fusion.139
  332.7 6.1 multiply_reduce_fusion.2
  338.8 6.2 multiply_convert_fusion.2
  344.9 3.0 fusion.85
  349.7 8.4 fusion.140
  358.1 9.0 fusion.2
  367.1 12.8 %multiply_reduce_fusion.1 = (f32[6,512]{1,0:T(8,128)S(1)}, f32[6,512,1536]{2,1,0:T(8,128)}) fusion(f32[6,512,1536]{2,1,0:T(8,128)} %get-tuple-element.251, f32[6,512]{1,0:T(8,128)S(1)} %log_add_fusion.1, bf16[512,6,64]{0,2,1:T(8,128)(2,1)} %bitcast.168, bf16[2048,6,192]{0,2,1:T(8,128)(2,1)} %copy-done.9), kind=kOutput, calls=%fused_computation.11 | convolution fusion | flops 618132480 | bytes 39346176 | tf_op jit(solution)/shard_map/qhd,khd->hqk/dot_general | solution.py:253
  379.9 12.9 %multiply_convert_fusion.1 = bf16[6,512,1536]{2,1,0:T(8,128)(2,1)S(1)} fusion(f32[6,512,1536]{2,1,0:T(8,128)} %get-tuple-element.257, f32[6,512,1536]{2,1,0:T(8,128)} %get-tuple-element.251, f32[6,512]{1,0:T(8,128)S(1)} %get-tuple-element.256, f32[6,512]{1,0:T(8,128)S(1)} %log_add_fusion.1), kind=kLoop, calls=%fused_computation.10 | loop fusion | flops 18874368 | bytes 47210496 | tf_op jit(solution)/shard_map/convert_element_type | solution.py:257
  392.8 3.9 fusion.84
  398.6 10.7 fusion.141
  409.3 10.5 fusion
  419.8 16.1 %multiply_reduce_fusion = (f32[6,512]{1,0:T(8,128)S(1)}, f32[6,512,2048]{2,1,0:T(8,128)}) fusion(f32[6,512,2048]{2,1,0:T(8,128)} %get-tuple-element.253, f32[6,512]{1,0:T(8,128)S(1)} %log_add_fusion, bf16[512,6,64]{0,2,1:T(8,128)(2,1)S(1)} %bitcast.166, bf16[2048,6,192]{0,2,1:T(8,128)(2,1)} %copy-done.9), kind=kOutput, calls=%fused_computation.2 | convolution fusion | flops 824177664 | bytes 52322304 | tf_op jit(solution)/shard_map/qhd,khd->hqk/dot_general | solution.py:253
  435.9 16.9 %multiply_convert_fusion = bf16[6,512,2048]{2,1,0:T(8,128)(2,1)S(1)} fusion(f32[6,512,2048]{2,1,0:T(8,128)} %get-tuple-element.255, f32[6,512,2048]{2,1,0:T(8,128)} %get-tuple-element.253, f32[6,512]{1,0:T(8,128)S(1)} %get-tuple-element.254, f32[6,512]{1,0:T(8,128)S(1)} %log_add_fusion), kind=kLoop, calls=%fused_computation.1 | loop fusion | flops 25165824 | bytes 62939136 | tf_op jit(solution)/shard_map/convert_element_type | solution.py:257
  452.9 4.5 copy-done.2
  457.3 6.1 fusion.83
  463.5 8.0 bitcast_add_fusion.1
  471.6 5.1 pad_maximum_fusion
  482.5 4.5 fusion.72
  487.1 6.4 fusion.67
  493.5 11.6 bitcast_add_fusion
  513.6 6.6 bitcast_convert_fusion
  520.1 9.3 fusion.89
  530.1 35.6 %multiply_convert_fusion.3 = (bf16[2048,1536]{1,0:T(8,128)(2,1)}, f32[2048,1536]{1,0:T(8,128)}, f32[2048,1536]{1,0:T(8,128)}) fusion(f32[1536]{0:T(1024)S(1)} %copy-done.64, bf16[2048,768]{1,0:T(8,128)(2,1)} %all-gather.11.cloned.1.call-done, bf16[768,1536]{1,0:T(8,128)(2,1)} %all-gather.13.cloned.1.call-done), kind=kOutput, calls=%fused_computation.26 | convolution fusion | flops 5039456256 | bytes 36968448 | tf_op jit(solution)/shard_map/dot_general | solution.py:213
  565.8 17.0 %convert_reduce_fusion = (f32[1536]{0:T(1024)S(1)}, bf16[2048,1536]{1,0:T(8,128)(2,1)S(1)}) fusion(f32[2048,1536]{1,0:T(8,128)} %get-tuple-element.212, bf16[2048,768]{1,0:T(8,128)(2,1)} %all-gather.17.cloned.1.call-done, bf16[768,1536]{1,0:T(8,128)(2,1)} %all-gather.15.cloned.1.call-done, f32[2048,1536]{1,0:T(8,128)} %get-tuple-element.245, ...), kind=kOutput, calls=%fused_computation.20 | convolution fusion | flops 4885314048 | bytes 36974592 | tf_op jit(solution)/shard_map/dot_general | solution.py:230
  585.4 6.4 convolution_convert_fusion
  592.5 8.0 fusion.88
  600.6 4.1 fusion.87
  604.7 11.1 fusion.90
  615.9 7.3 fusion.142
  623.2 3.7 add_convert_fusion.1
  627.0 3.3 fusion.111
  632.3 9.8 fusion.32
  642.2 9.9 fusion.143
  652.2 9.7 convolution_bitcast_fusion
  661.9 6.1 copy.72
  669.5 3.9 fusion.44
  673.4 3.3 fusion.49
  676.8 6.5 convert_reduce_fusion.5
  683.3 37.7 %all-reduce.25 = (f32[768]{0:T(1024)S(1)}, f32[768]{0:T(1024)S(1)}, f32[768]{0:T(1024)S(1)}, f32[768]{0:T(1024)S(1)}, f32[2304]{0:T(1024)S(1)}, /*index=5*/f32[768]{0:T(1024)S(1)}, f32[3072]{0:T(1024)S(1)}) all-reduce(f32[768]{0:T(1024)S(1)} %get-tuple-element.187, ...), channel_id=5, replica_groups=mesh['dp'=16,'tensor'=2] {'dp','tensor'}, use_global_device_ids=true, to_apply=%region_25.26.clone | all-reduce | flops 9216 | bytes 73728
  724.6 44.1 %reduce-scatter.18.cloned.1.call-done = f32[48,6,64]{2,0,1:T(8,128)} async-done(((f32[768,6,64]{2,0,1:T(8,128)}), f32[48,6,64]{2,0,1:T(8,128)}) %reduce-scatter.18.cloned.1.call-update) | async-done | bytes 73744 | tf_op jit(solution)/shard_map/reduce_scatter | solution.py:335
  768.7 141.9 %reduce-scatter.16.cloned.1.call-done = f32[48,6,192]{2,0,1:T(8,128)} async-done(((f32[768,6,192]{2,0,1:T(8,128)}), f32[48,6,192]{2,0,1:T(8,128)}) %reduce-scatter.16.cloned.1.call-update) | async-done | bytes 221200 | tf_op jit(solution)/shard_map/reduce_scatter | solution.py:334
  910.6 142.3 %reduce-scatter.20.cloned.1.call-done = f32[48,1536]{1,0:T(8,128)} async-done(((f32[768,1536]{1,0:T(8,128)}), f32[48,1536]{1,0:T(8,128)}) %reduce-scatter.20.cloned.1.call-update) | async-done | bytes 294928 | tf_op jit(solution)/shard_map/reduce_scatter | solution.py:336
  1052.9 141.6 %reduce-scatter.22.cloned.1.call-done = f32[48,1536]{1,0:T(8,128)} async-done(((f32[768,1536]{1,0:T(8,128)}), f32[48,1536]{1,0:T(8,128)}) %reduce-scatter.22.cloned.1.call-update) | async-done | bytes 294928
  (331 shorter events, 74.3 us)
Async XLA Ops:
  7.2 92.3 %copy-start.3 = (bf16[1024,768]{1,0:T(8,128)(2,1)S(1)}, bf16[1024,768]{1,0:T(8,128)(2,1)}, u32[]{:S(2)}) copy-start(bf16[1024,768]{1,0:T(8,128)(2,1)} %param.35) | copy-start | bytes 4718596
  7.2 288.3 %all-gather.17.cloned.1.call-start = ((), (), s32[]{:S(2)}) async-start(), calls=%async_computation.13 | async-start | bytes 4718592 | tf_op jit(solution)/shard_map/all_gather | solution.py:229
  7.9 292.2 %all-gather.9.cloned.1.call-start = ((), (), s32[]{:S(2)}) async-start(), calls=%async_computation.8 | async-start | bytes 2506752 | tf_op jit(solution)/shard_map/all_gather | solution.py:89
  8.7 294.3 %all-gather.7.cloned.1.call-start = ((), (), s32[]{:S(2)}) async-start(), calls=%async_computation.7 | async-start | bytes 4718592 | tf_op jit(solution)/shard_map/all_gather | solution.py:143
  97.8 5.5 copy-start.47
  97.8 5.5 copy-start.49
  103.3 426.2 %all-gather.11.cloned.1.call-start = ((), (), s32[]{:S(2)}) async-start(), calls=%async_computation.9 | async-start | bytes 4718592 | tf_op jit(solution)/shard_map/all_gather | solution.py:144
  103.9 425.6 %all-gather.13.cloned.1.call-start = ((), (), s32[]{:S(2)}) async-start(), calls=%async_computation.10 | async-start | bytes 2506752 | tf_op jit(solution)/shard_map/all_gather | solution.py:91
  104.5 461.3 %all-gather.15.cloned.1.call-start = ((), (), s32[]{:S(2)}) async-start(), calls=%async_computation.11 | async-start | bytes 2506752 | tf_op jit(solution)/shard_map/all_gather | solution.py:92
  104.6 57.8 %collective-permute-start = (bf16[48,6,64]{2,0,1:T(8,128)(2,1)S(1)}, bf16[48,6,64]{2,0,1:T(8,128)(2,1)S(1)}, u32[]{:S(2)}, u32[]{:S(2)}) collective-permute-start(bf16[48,6,64]{2,0,1:T(8,128)(2,1)S(1)} %copy-done.40), channel_id=1, source_target_pairs={{0,2},{2,4},{4,6},{6,8},{8,10},{10,12},{12,14},{14,16},{16,18},{18... | collective-permute-start | bytes 110600 | tf_op jit(solution)/shard_map/ppermute | solution.py:19
  105.1 564.3 %reduce-scatter.14.cloned.1.call-start = ((), (), s32[]{:S(2)}) async-start(), calls=%async_computation.15 | async-start | bytes 4718592 | tf_op jit(solution)/shard_map/reduce_scatter | solution.py:300
  154.4 155.5 %copy-start.32 = (f32[2048,16]{0,1:T(8,128)}, f32[2048,16]{0,1:T(8,128)S(1)}, u32[]{:S(2)}) copy-start(f32[2048,16]{0,1:T(8,128)S(1)} %get-tuple-element.237) | copy-start | bytes 393220
  154.4 155.5 %copy-start.34 = (f32[2048,16]{0,1:T(8,128)}, f32[2048,16]{0,1:T(8,128)S(1)}, u32[]{:S(2)}) copy-start(f32[2048,16]{0,1:T(8,128)S(1)} %get-tuple-element.238) | copy-start | bytes 393220
  162.4 9.6 collective-permute-start.1
  171.9 8.1 collective-permute-start.2
  180.1 9.0 collective-permute-start.3
  189.1 9.5 collective-permute-start.4
  198.6 7.9 collective-permute-start.5
  206.5 8.9 collective-permute-start.6
  215.4 8.5 collective-permute-start.7
  223.9 9.5 collective-permute-start.8
  233.4 7.9 collective-permute-start.9
  241.4 8.1 collective-permute-start.10
  249.5 9.1 collective-permute-start.11
  258.6 7.9 collective-permute-start.12
  266.6 7.9 collective-permute-start.13
  274.5 18.1 %collective-permute-start.14 = (bf16[48,6,64]{2,0,1:T(8,128)(2,1)S(1)}, bf16[48,6,64]{2,0,1:T(8,128)(2,1)S(1)}, u32[]{:S(2)}, u32[]{:S(2)}) collective-permute-start(bf16[48,6,64]{2,0,1:T(8,128)(2,1)S(1)} %collective-permute-done.13), channel_id=1, source_target_pairs={{0,2},{2,4},{4,6},{6,8},{8,10},{10,12},{12,14},{14,16},{16,18},{18... | collective-permute-start | bytes 110600 | tf_op jit(solution)/shard_map/ppermute | solution.py:19
  309.7 23.0 %copy-start.9 = (bf16[2048,6,192]{0,2,1:T(8,128)(2,1)}, bf16[2048,6,192]{0,2,1:T(8,128)(2,1)S(1)}, u32[]{:S(2)}) copy-start(bf16[2048,6,192]{0,2,1:T(8,128)(2,1)S(1)} %convert.33) | copy-start | bytes 14155780
  309.9 88.7 %copy-start.5 = (bf16[2048,6,48]{0,2,1:T(8,128)(2,1)}, bf16[2048,6,48]{0,2,1:T(8,128)(2,1)S(1)}, u32[]{:S(2)}) copy-start(bf16[2048,6,48]{0,2,1:T(8,128)(2,1)S(1)} %get-tuple-element.219) | copy-start | bytes 3538948
  312.7 7.2 copy-start.1
  330.0 8.8 copy-start
  332.7 6.1 copy-start.55
  349.7 8.4 copy-start.6
  398.5 10.7 copy-start.8
  409.2 10.5 copy-start.57
  409.2 10.5 copy-start.19
  419.7 16.2 %copy-start.59 = (f32[6,512]{1,0:T(8,128)}, f32[6,512]{1,0:T(8,128)S(1)}, u32[]{:S(2)}) copy-start(f32[6,512]{1,0:T(8,128)S(1)} %fusion) | copy-start | bytes 36868
  463.4 8.1 copy-start.14
  463.4 8.1 copy-start.15
  463.4 8.1 copy-start.16
  463.4 18.1 %slice-start = ((s8[12582912]{0:T(1024)(128)(4,1)}), s8[4194304]{0:T(1024)(128)(4,1)S(1)}, s32[]{:S(2)}) async-start(s8[12582912]{0:T(1024)(128)(4,1)} %bitcast.159), calls=%async_computation.20 | async-start | bytes 8388608
  463.4 18.1 %slice-start.1 = ((s8[12582912]{0:T(1024)(128)(4,1)}), s8[4194304]{0:T(1024)(128)(4,1)S(1)}, s32[]{:S(2)}) async-start(s8[12582912]{0:T(1024)(128)(4,1)} %bitcast.159), calls=%async_computation.21 | async-start | bytes 8388608
  463.5 23.6 %slice-start.3 = ((s8[18874368]{0:T(1024)(128)(4,1)}), s8[4194304]{0:T(1024)(128)(4,1)S(1)}, s32[]{:S(2)}) async-start(s8[18874368]{0:T(1024)(128)(4,1)} %bitcast.161), calls=%async_computation.23 | async-start | bytes 8388608
  463.5 23.6 %slice-start.4 = ((s8[18874368]{0:T(1024)(128)(4,1)}), s8[4194304]{0:T(1024)(128)(4,1)S(1)}, s32[]{:S(2)}) async-start(s8[18874368]{0:T(1024)(128)(4,1)} %bitcast.161), calls=%async_computation.24 | async-start | bytes 8388608
  471.5 5.2 copy-start.10
  471.6 15.5 %slice-start.5 = ((s8[18874368]{0:T(1024)(128)(4,1)}), s8[4194304]{0:T(1024)(128)(4,1)S(1)}, s32[]{:S(2)}) async-start(s8[18874368]{0:T(1024)(128)(4,1)} %bitcast.161), calls=%async_computation.25 | async-start | bytes 8388608
  478.3 8.7 slice-start.6
  487.1 6.4 copy-start.20
  493.5 11.6 copy-start.26
  529.4 140.0 %reduce-scatter.12.cloned.1.call-start = ((), (), s32[]{:S(2)}) async-start(), calls=%async_computation.14 | async-start | bytes 4718592 | tf_op jit(solution)/shard_map/reduce_scatter | solution.py:303
  565.8 19.6 %copy-start.68 = (bf16[768,1536]{1,0:T(8,128)(2,1)S(1)}, bf16[768,1536]{1,0:T(8,128)(2,1)}, u32[]{:S(2)}) copy-start(bf16[768,1536]{1,0:T(8,128)(2,1)} %all-gather.13.cloned.1.call-done) | copy-start | bytes 7077892
  591.8 8.7 copy-start.44
  591.8 8.7 copy-start.54
  591.8 84.9 %reduce-scatter.10.cloned.1.call-start = ((), (), s32[]{:S(2)}) async-start(), calls=%async_computation.12 | async-start | bytes 4718592 | tf_op jit(solution)/shard_map/reduce_scatter | solution.py:217
  604.7 11.1 copy-start.67
  615.9 7.3 copy-start.28
  615.9 7.3 copy-start.39
  626.9 141.8 %reduce-scatter.18.cloned.1.call-start = ((), (), s32[]{:S(2)}) async-start(), calls=%async_computation.17 | async-start | bytes 2506752 | tf_op jit(solution)/shard_map/reduce_scatter | solution.py:335
  632.3 278.4 %reduce-scatter.16.cloned.1.call-start = ((), (), s32[]{:S(2)}) async-start(), calls=%async_computation.16 | async-start | bytes 5013504 | tf_op jit(solution)/shard_map/reduce_scatter | solution.py:334
  642.2 410.7 %reduce-scatter.20.cloned.1.call-start = ((), (), s32[]{:S(2)}) async-start(), calls=%async_computation.18 | async-start | bytes 5013504 | tf_op jit(solution)/shard_map/reduce_scatter | solution.py:336
  652.1 542.4 %reduce-scatter.22.cloned.1.call-start = ((), (), s32[]{:S(2)}) async-start(), calls=%async_computation.19 | async-start | bytes 5013504
  668.1 5.3 copy-start.62
  668.1 5.3 copy-start.52
  721.7 473.3 %copy-start.70 = (f32[24]{0:T(128)}, f32[24]{0:T(128)S(1)}, u32[]{:S(2)}) copy-start(f32[24]{0:T(128)S(1)} %dynamic-slice.72) | copy-start | bytes 292
  (46 other events, 113.5 us)
Sparse Core Ops, SparseCore 0:
  9.6 14.8 all-gather.16
  27.1 64.8 all-gather.8
  103.4 7.9 all-gather.6
  112.9 13.2 all-gather.10
  128.8 66.1 all-gather.12
  197.6 65.1 all-gather.14
  529.6 6.7 reduce-scatter.13
  591.9 6.7 reduce-scatter.11
  627.1 6.7 reduce-scatter.9
  640.0 128.6 reduce-scatter.17
  774.5 136.1 reduce-scatter.15
  917.0 135.8 reduce-scatter.19
  1058.6 135.8 reduce-scatter.21
